TPU v7x, 32 devices: a whole 2x2x4 slice. The times are simulated.
32 devices in a mesh: fsdp: 8 (over y, x, core), tensor: 4 (over z).
Axes of the slice: x: 2, y: 2, z: 4, core: 2. Of those that a mesh axis runs over, the one named last changes fastest.
Arguments:
- hidden_t: bfloat16 [28672, 512], P('fsdp', 'tensor'), may hold values from -6 to 6
- down_weight: bfloat16 [28672, 4096], P('fsdp', 'tensor'), may hold values from -0.03125 to 0.03125
- probe: bfloat16 [28672, 4096], P('fsdp', 'tensor'), may hold values from -5 to 5
- grad_moment: bfloat16 [28672, 4096], P('fsdp', 'tensor'), may hold values from -0.0059814453 to 0.0059814453
- curv_moment: bfloat16 [28672, 4096], P('fsdp', 'tensor'), may hold values from 0.0099487305 to 0.099609375
- target: bfloat16 [512, 4096], P('fsdp', 'tensor'), may hold values from -6 to 6
Outputs:
- new_grad_moment: bfloat16 [28672, 4096], P('fsdp', 'tensor')
- new_curv_moment: bfloat16 [28672, 4096], P('fsdp', 'tensor')
- update: bfloat16 [28672, 4096], P('fsdp', 'tensor')
All inputs are finite; a program needn't handle non-finite values.
Results may differ from a plain program's by a relative error of at most 0.0056.
Values may be sent and summed in bfloat16 or wider, within the bound.
A program may use at most 192 MiB of HBM per device.

v0:
```python
import jax
import jax.numpy as jnp
from jax import lax
from jax.sharding import PartitionSpec as P

BETA_ONE = 0.965
BETA_TWO = 0.99
RHO_SCALE = 0.02
EPS_FLOOR = 0.0005


def cotangents(summed, target_rows, col_width, token_count):
    adjoint = ((summed[:, :col_width] - target_rows.astype(jnp.float32)) / token_count).astype(
        jnp.bfloat16
    )
    tangent_adjoint = (summed[:, col_width:] / token_count).astype(jnp.bfloat16)
    return jnp.concatenate([adjoint, tangent_adjoint], axis=1)


def shards(hidden_t, down_weight, probe, grad_moment, curv_moment, target):
    gathered = lax.all_gather(hidden_t, "tensor", axis=1, tiled=True)
    col_width = down_weight.shape[1]
    token_count = gathered.shape[1]
    paired = jnp.concatenate([down_weight, probe], axis=1)
    partial_out = lax.dot_general(
        gathered, paired, (((0,), (0,)), ((), ())), preferred_element_type=jnp.float32
    )
    totals = lax.psum(partial_out, "fsdp")
    target_all = lax.all_gather(target, "fsdp", axis=0, tiled=True)
    stacked = cotangents(totals, target_all, col_width, token_count)
    products = jnp.dot(gathered, stacked, preferred_element_type=jnp.float32)
    gradient = products[:, :col_width]
    hess_probe = products[:, col_width:]
    estimate = probe.astype(jnp.float32) * hess_probe
    moment_next = BETA_ONE * grad_moment.astype(jnp.float32) + (1.0 - BETA_ONE) * gradient
    curv_next = BETA_TWO * curv_moment.astype(jnp.float32) + (1.0 - BETA_TWO) * estimate
    raw_ratio = moment_next / jnp.maximum(RHO_SCALE * curv_next, EPS_FLOOR)
    update = jnp.clip(raw_ratio, -1.0, 1.0)
    return (
        moment_next.astype(jnp.bfloat16),
        curv_next.astype(jnp.bfloat16),
        update.astype(jnp.bfloat16),
    )


def solution(mesh):
    in_specs = (
        P("fsdp", "tensor"),
        P("fsdp", "tensor"),
        P("fsdp", "tensor"),
        P("fsdp", "tensor"),
        P("fsdp", "tensor"),
        P("fsdp", "tensor"),
    )
    out_specs = (P("fsdp", "tensor"), P("fsdp", "tensor"), P("fsdp", "tensor"))
    return jax.shard_map(shards, mesh=mesh, in_specs=in_specs, out_specs=out_specs, check_vma=False)
```

profile of v0, /device:TPU:0, one launch (start us, length us, event | category | flops | bytes accessed | tf_op | source)
XLA Modules:
  0.0 273.3 jit_solution(6230435863053550682)
XLA Ops:
  7.2 0.0 all-gather.3.cloned.1.call-start
  7.2 0.7 all-gather.3.cloned.1.call-update
  7.9 0.0 all-gather.5.cloned.1.call-start
  7.9 0.7 all-gather.5.cloned.1.call-update
  8.6 0.0 all-reduce.2.cloned.1.call-start
  8.7 75.6 %all-gather.3.cloned.1.call-done = bf16[3584,512]{1,0:T(8,128)(2,1)} async-done(((bf16[3584,128]{1,0:T(8,128)(2,1)}), bf16[3584,512]{1,0:T(8,128)(2,1)}) %all-gather.3.cloned.1.call-update) | async-done | bytes 3670032 | tf_op jit(solution)/shard_map/all_gather | solution.py:21
  84.3 16.0 %fusion.8 = f32[512,2048]{0,1:T(8,128)} fusion(bf16[3584,512]{1,0:T(8,128)(2,1)} %all-gather.3.cloned.1.call-done, bf16[3584,1024]{1,0:T(8,128)(2,1)} %param.8, bf16[3584,1024]{1,0:T(8,128)(2,1)} %param.7), kind=kOutput, calls=%fused_computation.12 | convolution fusion | flops 7545552896 | bytes 22544384 | tf_op jit(solution)/shard_map/dot_general | solution.py:25
  100.3 0.0 all-reduce.2.cloned.1.call-update
  100.3 10.2 %copy.19 = bf16[3584,1024]{0,1:T(8,128)(2,1)} copy(bf16[3584,1024]{1,0:T(8,128)(2,1)} %param.8) | data formatting | bytes 14680064 | tf_op args[2]
  110.6 10.2 %copy.16 = bf16[3584,1024]{0,1:T(8,128)(2,1)} copy(bf16[3584,1024]{1,0:T(8,128)(2,1)} %param.9) | data formatting | bytes 14680064 | tf_op args[3]
  120.7 10.0 %copy.18 = bf16[3584,1024]{0,1:T(8,128)(2,1)} copy(bf16[3584,1024]{1,0:T(8,128)(2,1)} %param.10) | data formatting | bytes 14680064 | tf_op args[4]
  130.8 0.0 all-gather.5.cloned.1.call-done
  130.8 1.5 copy.17
  132.3 59.9 %all-reduce.2.cloned.1.call-done = f32[512,2048]{0,1:T(8,128)} async-done(((f32[512,2048]{0,1:T(8,128)}), f32[512,2048]{0,1:T(8,128)}) %all-reduce.2.cloned.1.call-update) | async-done | bytes 4194320 | tf_op jit(solution)/shard_map/psum | solution.py:28
  192.2 0.0 slice-start
  192.2 3.0 %fusion.14 = (bf16[512,1024]{0,1:T(8,128)(2,1)S(1)}, bf16[512,1024]{0,1:T(8,128)(2,1)S(1)}) fusion(f32[512,2048]{0,1:T(8,128)} %all-reduce.2.cloned.1.call-done, bf16[512,1024]{0,1:T(8,128)(2,1)S(1)} %copy.17), kind=kLoop, calls=%fused_computation.18 | loop fusion | flops 3145728 | bytes 7340032 | tf_op jit(solution)/shard_map/convert_element_type | solution.py:13
  195.2 0.0 slice-start.1
  195.3 16.8 %convolution_bitcast_fusion = f32[3584,2048]{0,1:T(8,128)} fusion(bf16[3584,512]{1,0:T(8,128)(2,1)} %all-gather.3.cloned.1.call-done, bf16[512,1024]{0,1:T(8,128)(2,1)S(1)} %get-tuple-element.13, bf16[512,1024]{0,1:T(8,128)(2,1)S(1)} %get-tuple-element.12), kind=kOutput, calls=%fused_computation | convolution fusion | flops 7520387072 | bytes 35127296 | tf_op jit(solution)/shard_map/dot_general | solution.py:31
  212.1 0.0 slice-done
  212.1 0.0 slice-done.1
  212.1 23.6 %clamp_convert_fusion = (bf16[3584,1024]{0,1:T(8,128)(2,1)}, bf16[3584,1024]{0,1:T(8,128)(2,1)}, bf16[3584,1024]{0,1:T(8,128)(2,1)}) fusion(f32[3584,2048]{0,1:T(8,128)} %convolution_bitcast_fusion, bf16[3584,1024]{0,1:T(8,128)(2,1)} %copy.16, bf16[3584,1024]{0,1:T(8,128)(2,1)S(1)} %bitcast.7, bf16[3584,1024]{0,1:T(8,128)(2,1)} %copy.18), kind=kLoop, calls=%fused_computation.10 | loop fusion | flops 62390272 | bytes 73400320 | tf_op jit(solution)/shard_map/convert_element_type | solution.py:42
  235.6 10.4 %copy.20 = bf16[3584,1024]{1,0:T(8,128)(2,1)} copy(bf16[3584,1024]{0,1:T(8,128)(2,1)} %get-tuple-element.11) | data formatting | bytes 14680064
  246.0 10.4 %copy.21 = bf16[3584,1024]{1,0:T(8,128)(2,1)} copy(bf16[3584,1024]{0,1:T(8,128)(2,1)} %get-tuple-element.10) | data formatting | bytes 14680064
  256.4 10.4 %copy.22 = bf16[3584,1024]{1,0:T(8,128)(2,1)} copy(bf16[3584,1024]{0,1:T(8,128)(2,1)} %get-tuple-element.9) | data formatting | bytes 14680064
  (1 shorter events, 0.0 us)
Async XLA Ops:
  7.2 77.1 %all-gather.3.cloned.1.call-start = ((), (), s32[]{:S(2)}) async-start(), calls=%async_computation | async-start | bytes 4587520 | tf_op jit(solution)/shard_map/all_gather | solution.py:21
  7.9 122.9 %all-gather.5.cloned.1.call-start = ((), (), s32[]{:S(2)}) async-start(), calls=%async_computation.2 | async-start | bytes 1179648 | tf_op jit(solution)/shard_map/all_gather | solution.py:29
  8.6 183.6 %all-reduce.2.cloned.1.call-start = ((), (), s32[]{:S(2)}) async-start(), calls=%async_computation.1 | async-start | bytes 8388608 | tf_op jit(solution)/shard_map/psum | solution.py:28
  192.2 19.9 %slice-start = ((s8[7340032]{0:T(1024)(128)(4,1)}), s8[4194304]{0:T(1024)(128)(4,1)S(1)}, s32[]{:S(2)}) async-start(s8[7340032]{0:T(1024)(128)(4,1)} %bitcast.6), calls=%async_computation.3 | async-start | bytes 8388608
  195.2 16.8 %slice-start.1 = ((s8[7340032]{0:T(1024)(128)(4,1)}), s8[3145728]{0:T(1024)(128)(4,1)S(1)}, s32[]{:S(2)}) async-start(s8[7340032]{0:T(1024)(128)(4,1)} %bitcast.6), calls=%async_computation.4 | async-start | bytes 6291456
Sparse Core Ops, SparseCore 0:
  9.6 74.6 all-gather.2
  86.2 21.6 all-gather.4
  111.2 80.9 all-reduce.1
where the time goes:
time: 275 us; the launch traced here: 273 us
  waiting for transfers between devices  137 us (50%)
  local copies, waits for them, and re-layouts  63.2 us (23%)
  matrix products  32.8 us (12%)
  other arithmetic  26.6 us (10%)
  between operations  13.8 us (5%)
    all_gather x1, waiting for transfers between devices, shards(): gathered = lax.all_gather(hidden_t, 'tensor', axis=1, tiled=True)  75.6 us
    unnamed x10, local copies, waits for them, and re-layouts  61.7 us
    psum x1, waiting for transfers between devices, shards(): totals = lax.psum(partial_out, 'fsdp')  59.9 us
    convert_element_type x1, other arithmetic, shards(): update.astype(jnp.bfloat16)  23.6 us
    dot_general x1, matrix products, shards(): products = jnp.dot(gathered, stacked, preferred_element_type=jnp.float32)  16.8 us
    dot_general x1, matrix products, shards(): lax.dot_general(gathered, paired, (((0,), (0,)), ((), ())), preferred_ele...  16 us
  transfers between devices with their start and end apart: 3, of which 2 were waited for; matrix products, arithmetic and copies ran while one was open for 18% of the time, Pallas kernels for 0%

commit v1 on v0

--- a/solution.py
+++ b/solution.py
@@ -25,7 +25,9 @@
     partial_out = lax.dot_general(
         gathered, paired, (((0,), (0,)), ((), ())), preferred_element_type=jnp.float32
     )
-    totals = lax.psum(partial_out, "fsdp")
+    totals = partial_out
+    for hop in (1, 2, 4):
+        totals = totals + lax.ppermute(totals, "fsdp", [(dev, dev ^ hop) for dev in range(8)])
     target_all = lax.all_gather(target, "fsdp", axis=0, tiled=True)
     stacked = cotangents(totals, target_all, col_width, token_count)
     products = jnp.dot(gathered, stacked, preferred_element_type=jnp.float32)

time: 275 us -> 384 us (1.40)
  waiting for transfers between devices: 137 us -> 239 us
  other arithmetic: 26.6 us -> 32.7 us
    ppermute x0 -> x3, waiting for transfers between devices: none -> 162 us  [shards(): lax.ppermute(totals, 'fsdp', [(dev, dev ^ hop) for dev in range(8)])]
    psum x1 -> x0, waiting for transfers between devices: 59.9 us -> none  [shards(): totals = lax.psum(partial_out, 'fsdp')]
    add x0 -> x3, other arithmetic: none -> 8.46 us  [shards(): totals + lax.ppermute(totals, 'fsdp', [(dev, dev ^ hop) for dev in range(...]
    dot_general x1, matrix products: 16 us -> 12.2 us  [shards(): lax.dot_general(gathered, paired, (((0,), (0,)), ((), ())), preferred_ele...]
  transfers between devices with their start and end apart: 3 -> 5, of which waited for: 2 -> 4; matrix products, arithmetic and copies ran while one was open for 18% -> 8% of each run, Pallas kernels for 0% -> 0%
where the time goes in v1:
time: 384 us; the launch traced here: 382 us
  waiting for transfers between devices  239 us (62%)
  local copies, waits for them, and re-layouts  62.5 us (16%)
  other arithmetic  32.7 us (9%)
  matrix products  29.4 us (8%)
  between operations  15.5 us (4%)
    ppermute x3, waiting for transfers between devices, shards(): lax.ppermute(totals, 'fsdp', [(dev, dev ^ hop) for dev in range(8)])  162 us
    all_gather x1, waiting for transfers between devices, shards(): gathered = lax.all_gather(hidden_t, 'tensor', axis=1, tiled=True)  76.3 us
    unnamed x10, local copies, waits for them, and re-layouts  61 us
    convert_element_type x1, other arithmetic, shards(): update.astype(jnp.bfloat16)  23.6 us
    dot_general x1, matrix products, shards(): products = jnp.dot(gathered, stacked, preferred_element_type=jnp.float32)  17.3 us
    dot_general x1, matrix products, shards(): lax.dot_general(gathered, paired, (((0,), (0,)), ((), ())), preferred_ele...  12.2 us
    add x3, other arithmetic, shards(): totals + lax.ppermute(totals, 'fsdp', [(dev, dev ^ hop) for dev in range(...  8.46 us
  transfers between devices with their start and end apart: 5, of which 4 were waited for; matrix products, arithmetic and copies ran while one was open for 8% of the time, Pallas kernels for 0%

profile of v1, /device:TPU:0, one launch (start us, length us, event | category | flops | bytes accessed | tf_op | source)
XLA Modules:
  0.0 382.2 jit_solution(8380507689736515942)
XLA Ops:
  8.0 0.0 all-gather.3.cloned.1.call-start
  8.0 0.7 all-gather.3.cloned.1.call-update
  8.7 0.0 all-gather.5.cloned.1.call-start
  8.8 76.3 %all-gather.3.cloned.1.call-done = bf16[3584,512]{1,0:T(8,128)(2,1)} async-done(((bf16[3584,128]{1,0:T(8,128)(2,1)}), bf16[3584,512]{1,0:T(8,128)(2,1)}) %all-gather.3.cloned.1.call-update) | async-done | bytes 3670032 | tf_op jit(solution)/shard_map/all_gather | solution.py:21
  85.1 12.2 %fusion.8 = f32[512,2048]{0,1:T(8,128)S(1)} fusion(bf16[3584,512]{1,0:T(8,128)(2,1)} %all-gather.3.cloned.1.call-done, bf16[3584,1024]{1,0:T(8,128)(2,1)} %param.8, bf16[3584,1024]{1,0:T(8,128)(2,1)} %param.7), kind=kOutput, calls=%fused_computation.12 | convolution fusion | flops 7545552896 | bytes 22544384 | tf_op jit(solution)/shard_map/dot_general | solution.py:25
  97.3 0.1 collective-permute-start
  97.4 7.1 %collective-permute-done = f32[512,2048]{0,1:T(8,128)S(1)} collective-permute-done((f32[512,2048]{0,1:T(8,128)S(1)}, f32[512,2048]{0,1:T(8,128)S(1)}, u32[]{:S(2)}, u32[]{:S(2)}) %collective-permute-start) | collective-permute-done | bytes 4194336 | tf_op jit(solution)/shard_map/ppermute | solution.py:30
  104.5 1.0 add.15
  105.5 1.5 collective-permute-start.1
  107.1 91.1 %collective-permute-done.1 = f32[512,2048]{0,1:T(8,128)S(1)} collective-permute-done((f32[512,2048]{0,1:T(8,128)S(1)}, f32[512,2048]{0,1:T(8,128)S(1)}, u32[]{:S(2)}, u32[]{:S(2)}) %collective-permute-start.1) | collective-permute-done | bytes 4194336 | tf_op jit(solution)/shard_map/ppermute | solution.py:30
  198.2 3.0 add.16
  201.2 1.5 collective-permute-start.2
  202.6 0.0 all-gather.5.cloned.1.call-update
  202.7 9.9 %copy.19 = bf16[3584,1024]{0,1:T(8,128)(2,1)} copy(bf16[3584,1024]{1,0:T(8,128)(2,1)} %param.8) | data formatting | bytes 14680064 | tf_op args[2]
  212.6 9.9 %copy.16 = bf16[3584,1024]{0,1:T(8,128)(2,1)} copy(bf16[3584,1024]{1,0:T(8,128)(2,1)} %param.9) | data formatting | bytes 14680064 | tf_op args[3]
  222.5 9.9 %copy.18 = bf16[3584,1024]{0,1:T(8,128)(2,1)} copy(bf16[3584,1024]{1,0:T(8,128)(2,1)} %param.10) | data formatting | bytes 14680064 | tf_op args[4]
  232.5 0.0 all-gather.5.cloned.1.call-done
  232.5 1.5 copy.17
  234.0 63.5 %collective-permute-done.2 = f32[512,2048]{0,1:T(8,128)} collective-permute-done((f32[512,2048]{0,1:T(8,128)}, f32[512,2048]{0,1:T(8,128)}, u32[]{:S(2)}, u32[]{:S(2)}) %collective-permute-start.2) | collective-permute-done | bytes 4194336 | tf_op jit(solution)/shard_map/ppermute | solution.py:30
  297.5 4.5 %add.17 = f32[512,2048]{0,1:T(8,128)S(1)} add(f32[512,2048]{0,1:T(8,128)} %add.16, f32[512,2048]{0,1:T(8,128)} %collective-permute-done.2) | non-fusion elementwise | flops 1048576 | bytes 12582912 | tf_op jit(solution)/shard_map/add | solution.py:30
  302.0 0.0 slice-start
  302.0 0.7 fusion.14
  302.7 0.0 slice-start.1
  302.7 17.3 %convolution_bitcast_fusion = f32[3584,2048]{0,1:T(8,128)} fusion(bf16[3584,512]{1,0:T(8,128)(2,1)} %all-gather.3.cloned.1.call-done, bf16[512,1024]{0,1:T(8,128)(2,1)S(1)} %get-tuple-element.13, bf16[512,1024]{0,1:T(8,128)(2,1)S(1)} %get-tuple-element.12), kind=kOutput, calls=%fused_computation | convolution fusion | flops 7520387072 | bytes 35127296 | tf_op jit(solution)/shard_map/dot_general | solution.py:33
  320.0 0.0 slice-done
  320.0 0.0 slice-done.1
  320.0 23.6 %clamp_convert_fusion = (bf16[3584,1024]{0,1:T(8,128)(2,1)}, bf16[3584,1024]{0,1:T(8,128)(2,1)}, bf16[3584,1024]{0,1:T(8,128)(2,1)}) fusion(f32[3584,2048]{0,1:T(8,128)} %convolution_bitcast_fusion, bf16[3584,1024]{0,1:T(8,128)(2,1)} %copy.16, bf16[3584,1024]{0,1:T(8,128)(2,1)S(1)} %bitcast.7, bf16[3584,1024]{0,1:T(8,128)(2,1)} %copy.18), kind=kLoop, calls=%fused_computation.10 | loop fusion | flops 62390272 | bytes 73400320 | tf_op jit(solution)/shard_map/convert_element_type | solution.py:44
  343.6 10.4 %copy.20 = bf16[3584,1024]{1,0:T(8,128)(2,1)} copy(bf16[3584,1024]{0,1:T(8,128)(2,1)} %get-tuple-element.11) | data formatting | bytes 14680064
  354.0 10.4 %copy.21 = bf16[3584,1024]{1,0:T(8,128)(2,1)} copy(bf16[3584,1024]{0,1:T(8,128)(2,1)} %get-tuple-element.10) | data formatting | bytes 14680064
  364.3 10.4 %copy.22 = bf16[3584,1024]{1,0:T(8,128)(2,1)} copy(bf16[3584,1024]{0,1:T(8,128)(2,1)} %get-tuple-element.9) | data formatting | bytes 14680064
  (1 shorter events, 0.0 us)
Async XLA Ops:
  8.0 77.1 %all-gather.3.cloned.1.call-start = ((), (), s32[]{:S(2)}) async-start(), calls=%async_computation | async-start | bytes 4587520 | tf_op jit(solution)/shard_map/all_gather | solution.py:21
  8.7 223.7 %all-gather.5.cloned.1.call-start = ((), (), s32[]{:S(2)}) async-start(), calls=%async_computation.1 | async-start | bytes 1179648 | tf_op jit(solution)/shard_map/all_gather | solution.py:31
  97.3 7.2 %collective-permute-start = (f32[512,2048]{0,1:T(8,128)S(1)}, f32[512,2048]{0,1:T(8,128)S(1)}, u32[]{:S(2)}, u32[]{:S(2)}) collective-permute-start(f32[512,2048]{0,1:T(8,128)S(1)} %fusion.8), channel_id=1, source_target_pairs={{0,4},{4,0},{8,12},{12,8},{16,20},{20,16},{24,28},{28,24},{1,5},{5... | collective-permute-start | bytes 12582920 | tf_op jit(solution)/shard_map/ppermute | solution.py:30
  105.5 92.7 %collective-permute-start.1 = (f32[512,2048]{0,1:T(8,128)S(1)}, f32[512,2048]{0,1:T(8,128)S(1)}, u32[]{:S(2)}, u32[]{:S(2)}) collective-permute-start(f32[512,2048]{0,1:T(8,128)S(1)} %add.15), channel_id=1, source_target_pairs={{0,8},{4,12},{8,0},{12,4},{16,24},{20,28},{24,16},{28,20},{1,9},{5... | collective-permute-start | bytes 12582920 | tf_op jit(solution)/shard_map/ppermute | solution.py:30
  201.2 96.3 %collective-permute-start.2 = (f32[512,2048]{0,1:T(8,128)}, f32[512,2048]{0,1:T(8,128)}, u32[]{:S(2)}, u32[]{:S(2)}) collective-permute-start(f32[512,2048]{0,1:T(8,128)} %add.16), channel_id=1, source_target_pairs={{0,16},{4,20},{8,24},{12,28},{16,0},{20,4},{24,8},{28,12},{1,17},{... | collective-permute-start | bytes 12582920 | tf_op jit(solution)/shard_map/ppermute | solution.py:30
  302.0 18.0 %slice-start = ((s8[7340032]{0:T(1024)(128)(4,1)}), s8[4194304]{0:T(1024)(128)(4,1)S(1)}, s32[]{:S(2)}) async-start(s8[7340032]{0:T(1024)(128)(4,1)} %bitcast.6), calls=%async_computation.2 | async-start | bytes 8388608
  302.7 17.3 %slice-start.1 = ((s8[7340032]{0:T(1024)(128)(4,1)}), s8[3145728]{0:T(1024)(128)(4,1)S(1)}, s32[]{:S(2)}) async-start(s8[7340032]{0:T(1024)(128)(4,1)} %bitcast.6), calls=%async_computation.3 | async-start | bytes 6291456
Sparse Core Ops, SparseCore 0:
  10.4 74.6 all-gather.2
Sparse Core Ops, SparseCore 1:
  202.7 25.0 all-gather.4
